TPU v7x, 32 devices: a whole 2x2x4 slice. The times are simulated.
32 devices in a mesh: seq: 8 (over z, x), doc: 4 (over y, core).
Axes of the slice: x: 2, y: 2, z: 4, core: 2. Of those that a mesh axis runs over, the one named last changes fastest.
Arguments:
- inputs: bfloat16 [4096, 1024], P('seq', 'doc'), may hold values from -4 to 4
- queries: bfloat16 [4096, 1024], P('seq', 'doc'), may hold values from -128 to 128
- keys_values: bfloat16 [2, 4096, 1024], P(None, 'seq', 'doc'), may hold values from -10 to 10
- slot_weight: bfloat16 [1024, 4096], P(None, 'doc'), may hold values from -3 to 3
- slot_gain: float32 [2, 1024], P(None, 'doc'), may hold values from 0.1 to 1.9
- slot_bias: float32 [2, 1024], P(None, 'doc'), may hold values from -3 to 3
- bounds: int32 [2, 4096], P(None, 'seq'), may hold values from 0 to 4096, as said below
Outputs:
- attended: bfloat16 [4096, 1024], P('seq', 'doc')
Inputs may be any that keep to these rules, and one draw needn't show every extreme that they name: The sequence holds exactly 2 documents in order, the first starting at 0 and each of 1024 tokens or more: bounds[0, i] <= i < bounds[1, i], and every token of a document has the same pair.
All inputs are finite; a program needn't handle non-finite values.
Results may differ from a plain program's by a relative error of at most 0.0045.
Values may be sent and summed in bfloat16 or wider, within the bound.
A program may use at most 64 MiB of HBM per device.

v0:
```python
import jax
import jax.numpy as jnp
from jax import lax
from jax.sharding import PartitionSpec as P

DH = 64
R = 256
W = 128
DOCS = 2


epsilon = 1e-05


def extended(array, sides, width):
    for axis, dim in sides:
        devices, length = (lax.axis_size(axis), array.shape[dim])
        up = [(i, (i + 1) % devices) for i in range(devices - 1)]
        down = [(j, i) for i, j in up]
        last = lax.slice_in_dim(array, length - width, length, axis=dim)
        first = lax.slice_in_dim(array, 0, width, axis=dim)
        before = lax.ppermute(last, axis, up)
        after = lax.ppermute(first, axis, down)
        array = jnp.concatenate([before, array, after], axis=dim)
    return array


def normalize(numerator, gain, bias):
    mean_val = jnp.mean(numerator, axis=-1, keepdims=True)
    centred = numerator - mean_val
    variance = jnp.mean(centred * centred, axis=-1, keepdims=True)
    return centred * lax.rsqrt(variance + epsilon) * gain + bias


def attend(query_block, window, lower, upper, first_pos, slot_keys, slot_values):
    q_len = query_block.shape[0]
    k_len = window.shape[1]
    second = (lower > 0)[None, :, None]
    near_scores = (
        jnp.einsum("qhe,khe->hqk", query_block, window[0], preferred_element_type=jnp.float32)
        * 0.125
    )
    far_all = (
        jnp.einsum("qhe,ghre->ghqr", query_block, slot_keys, preferred_element_type=jnp.float32)
        * 0.125
    )
    far_scores = jnp.where(second, far_all[1], far_all[0])
    query_pos = first_pos + jnp.arange(q_len, dtype=jnp.int32)
    key_pos = first_pos - W + jnp.arange(k_len, dtype=jnp.int32)
    offset = key_pos[None, :] - query_pos[:, None]
    allowed = (
        (jnp.abs(offset) <= W)
        & (key_pos[None, :] >= lower[:, None])
        & (key_pos[None, :] < upper[:, None])
    )
    near_scores = jnp.where(allowed[None], near_scores, -jnp.inf)
    row_top = jnp.maximum(jnp.max(near_scores, axis=-1), jnp.max(far_scores, axis=-1))
    near_weight = jnp.exp(near_scores - row_top[..., None])
    far_weight = jnp.exp(far_scores - row_top[..., None])
    row_total = jnp.sum(near_weight, axis=-1) + jnp.sum(far_weight, axis=-1)
    far_b = far_weight.astype(jnp.bfloat16)
    zero_val = jnp.zeros((), jnp.bfloat16)
    result = jnp.einsum(
        "hqk,khe->qhe",
        near_weight.astype(jnp.bfloat16),
        window[1],
        preferred_element_type=jnp.float32,
    )
    result = result + jnp.einsum(
        "hqr,hre->qhe",
        jnp.where(second, zero_val, far_b),
        slot_values[0],
        preferred_element_type=jnp.float32,
    )
    result = result + jnp.einsum(
        "hqr,hre->qhe",
        jnp.where(second, far_b, zero_val),
        slot_values[1],
        preferred_element_type=jnp.float32,
    )
    result = result / jnp.transpose(row_total)[:, :, None]
    return result.reshape(q_len, -1).astype(jnp.bfloat16)


def on_device(inputs, queries, keys_values, slot_weight, slot_gain, slot_bias, bounds):
    tok_rows = inputs.shape[0]
    local_heads = queries.shape[1] // DH
    owner = bounds[0] > 0
    logits = jnp.dot(
        lax.all_gather(inputs, "doc", axis=1, tiled=True),
        slot_weight,
        preferred_element_type=jnp.float32,
    )
    first_top = jnp.max(jnp.where(owner[:, None], -jnp.inf, logits), axis=0)
    other_top = jnp.max(jnp.where(owner[:, None], logits, -jnp.inf), axis=0)
    slot_top = lax.pmax(jnp.stack([first_top, other_top]), "seq")
    top_rows = jnp.where(owner[:, None], slot_top[1][None, :], slot_top[0][None, :])
    proj = jnp.exp(logits - top_rows).astype(jnp.bfloat16).reshape(tok_rows, local_heads, R)
    zero_val = jnp.zeros((), jnp.bfloat16)
    split_proj = jnp.stack(
        [
            jnp.where(owner[:, None, None], zero_val, proj),
            jnp.where(owner[:, None, None], proj, zero_val),
        ]
    )
    kv_pair = keys_values.reshape(2, tok_rows, local_heads, DH)
    numerator = jnp.einsum(
        "gthr,stha->ghrsa", split_proj, kv_pair, preferred_element_type=jnp.float32
    )
    numerator = numerator.reshape(DOCS * local_heads * R, 2 * DH)
    gain_rows = jnp.broadcast_to(
        jnp.transpose(slot_gain.reshape(2, local_heads, DH), (1, 0, 2))[None, :, None],
        (DOCS, local_heads, R, 2, DH),
    ).reshape(DOCS * local_heads * R, 2, DH)
    bias_rows = jnp.broadcast_to(
        jnp.transpose(slot_bias.reshape(2, local_heads, DH), (1, 0, 2))[None, :, None],
        (DOCS, local_heads, R, 2, DH),
    ).reshape(DOCS * local_heads * R, 2, DH)
    summed = lax.psum(numerator, "seq")
    slot_table = normalize(
        summed.reshape(DOCS * local_heads * R, 2, DH), gain_rows, bias_rows
    ).astype(jnp.bfloat16)
    slot_table = slot_table.reshape(DOCS, local_heads, R, 2, DH)
    slot_keys = slot_table[:, :, :, 0]
    slot_values = slot_table[:, :, :, 1]
    kv_rims = extended(keys_values, (("seq", 1),), W)
    block_len = min(512, tok_rows)
    root = lax.axis_index("seq") * tok_rows
    query_block = queries.reshape(block_len, local_heads, DH)
    window = kv_rims.reshape(2, block_len + 2 * W, local_heads, DH)
    lower = bounds[0, 0:block_len]
    upper = bounds[1, 0:block_len]
    pieces = attend(query_block, window, lower, upper, root + 0, slot_keys, slot_values)
    return pieces


def solution(mesh):
    return jax.shard_map(
        on_device,
        mesh=mesh,
        in_specs=(
            P("seq", "doc"),
            P("seq", "doc"),
            P(None, "seq", "doc"),
            P(None, "doc"),
            P(None, "doc"),
            P(None, "doc"),
            P(None, "seq"),
        ),
        out_specs=P("seq", "doc"),
        check_vma=False,
    )
```

profile of v0, /device:TPU:0, one launch (start us, length us, event | category | flops | bytes accessed | tf_op | source)
XLA Modules:
  0.0 162.6 jit_solution(9959589010399088472)
XLA Ops:
  6.5 0.7 all-gather.2.cloned.1.call-update
  7.3 1.7 %fusion.45 = (bf16[2,128,256]{2,1,0:T(8,128)(2,1)}, bf16[2,128,256]{2,1,0:T(8,128)(2,1)}) fusion(bf16[2,512,256]{2,1,0:T(8,128)(2,1)} %param.9), kind=kLoop, calls=%fused_computation.69 | loop fusion | bytes 524288 | tf_op jit(solution)/shard_map/slice | solution.py:21
  9.0 1.3 collective-permute-start.1
  10.3 6.1 %collective-permute-start = (bf16[2,128,256]{2,1,0:T(8,128)(2,1)}, bf16[2,128,256]{2,1,0:T(8,128)(2,1)}, u32[]{:S(2)}, u32[]{:S(2)}) collective-permute-start(bf16[2,128,256]{2,1,0:T(8,128)(2,1)} %get-tuple-element.14), channel_id=1, source_target_pairs={{0,4},{4,8},{8,12},{12,16},{16,20},{20,24},{24,28},{1,5},{5,9},{9,... | collective-permute-start | bytes 393224 | tf_op jit(solution)/shard_map/ppermute | solution.py:22
  16.5 2.1 %copy.25 = bf16[2,512,256]{1,2,0:T(8,128)(2,1)} copy(bf16[2,512,256]{2,1,0:T(8,128)(2,1)} %param.9) | data formatting | bytes 1048576 | tf_op args[2]
  18.5 0.8 fusion.47
  19.3 9.2 %all-gather.2.cloned.1.call-done = bf16[512,1024]{1,0:T(8,128)(2,1)} async-done(((bf16[512,256]{1,0:T(8,128)(2,1)}), bf16[512,1024]{1,0:T(8,128)(2,1)}) %all-gather.2.cloned.1.call-update) | async-done | bytes 1048592 | tf_op jit(solution)/shard_map/all_gather | solution.py:90
  28.5 3.9 %select_reduce_fusion.1 = (f32[1024]{0:T(1024)S(1)}, f32[1024]{0:T(1024)S(1)}, f32[512,1024]{1,0:T(8,128)}) fusion(pred[512]{0:T(512)(128)(4,1)S(1)} %broadcast_compare_fusion, bf16[512,1024]{1,0:T(8,128)(2,1)} %all-gather.2.cloned.1.call-done, bf16[1024,1024]{1,0:T(8,128)(2,1)S(1)} %copy-done), kind=kOutput, calls=%fused_computation.18 | convolution fusion | flops 1075836928 | bytes 5251584 | tf_op jit(solution)/shard_map/dot_general | solution.py:89
  32.4 21.6 %pmax.7 = f32[2,1024]{1,0:T(2,128)S(1)} all-reduce(f32[2,1024]{1,0:T(2,128)S(1)} %pad_maximum_fusion), channel_id=1, replica_groups=mesh['seq'=8,'doc'=4] {'seq'}, use_global_device_ids=true, to_apply=%region_3.4 | all-reduce | flops 2048 | bytes 16384 | tf_op jit(solution)/shard_map/pmax | solution.py:96
  54.0 2.0 %exponential_convert_fusion = bf16[512,1024]{1,0:T(8,128)(2,1)S(1)} fusion(f32[512,1024]{1,0:T(8,128)} %get-tuple-element.19, f32[1024]{0:T(1024)S(1)} %bitcast.104, f32[1024]{0:T(1024)S(1)} %bitcast.103, pred[512]{0:T(512)(128)(4,1)S(1)} %broadcast_compare_fusion), kind=kLoop, calls=%fused_computation.16 | loop fusion | flops 1572864 | bytes 3154432 | tf_op jit(solution)/shard_map/convert_element_type | solution.py:98
  56.0 1.6 reshape.202
  57.6 1.5 broadcast_select_fusion.1
  59.6 0.7 copy.27
  60.3 1.5 reshape.204
  64.1 1.0 constant_dynamic-update-slice_fusion.2
  65.2 0.9 constant_dynamic-update-slice_fusion
  66.1 0.8 fusion.44
  66.9 1.0 copy.20
  67.9 1.2 copy.21
  69.0 4.5 %fusion.2 = (f32[4,512]{1,0:T(4,128)}, f32[4,768,512]{2,1,0:T(8,128)}) fusion(pred[512,768]{0,1:T(8,128)(4,1)S(1)} %fusion.13, bf16[768,4,64]{0,2,1:T(8,128)(2,1)S(1)} %bitcast.95, bf16[512,4,64]{0,2,1:T(8,128)(2,1)S(1)} %bitcast.93), kind=kOutput, calls=%fused_computation.4 | convolution fusion | flops 206043136 | bytes 7348224 | tf_op jit(solution)/shard_map/qhe,khe->hqk/dot_general | solution.py:40
  73.5 62.8 %all-reduce.2.cloned.1.call-done = f32[2048,128]{0,1:T(8,128)} async-done(((f32[2048,128]{0,1:T(8,128)}), f32[2048,128]{0,1:T(8,128)}) %all-reduce.2.cloned.1.call-update) | async-done | bytes 1048592 | tf_op jit(solution)/shard_map/psum | solution.py:119
  136.3 1.4 bitcast_reduce_fusion
  138.3 1.3 copy.28
  139.7 1.4 fusion.22
  141.7 1.3 rsqrt.12
  143.0 1.3 copy.30
  144.3 1.7 %reshape.205 = f32[2,4,256,2,64]{2,1,0,4,3:T(4,128)} reshape(f32[2048,128]{0,1:T(8,128)S(1)} %copy-done.1) | data formatting | bytes 2097152 | tf_op jit(solution)/shard_map/reshape | solution.py:121
  146.0 1.6 %fusion.26 = bf16[2,4,256,2,64]{2,4,0,1,3:T(8,128)(2,1)S(1)} fusion(f32[2,4,256,2,64]{2,1,0,4,3:T(4,128)} %reshape.205, f32[4,2,64]{2,0,1:T(4,128)} %bitcast.102, f32[4,2,64]{2,0,1:T(4,128)} %bitcast.101, f32[2,4,256,2]{2,0,1,3:T(2,128)} %copy.30, f32[2,4,256,2]{2,0,1,3:T(2,128)S(1)} %copy-done.7), kind=kLoop, calls=%fused_computation.38 | loop fusion | flops 1310720 | bytes 1609728 | tf_op jit(solution)/shard_map/convert_element_type | solution.py:122
  147.7 1.9 %multiply_bitcast_fusion = f32[2,4,512,256]{2,3,0,1:T(8,128)S(1)} fusion(bf16[512,4,64,1]{0,2,3,1:T(8,128)(2,1)} %bitcast.94, bf16[2,4,256,2,64]{2,4,0,1,3:T(8,128)(2,1)S(1)} %fusion.26), kind=kOutput, calls=%fused_computation.5 | convolution fusion | flops 135266304 | bytes 4718592 | tf_op jit(solution)/shard_map/qhe,ghre->ghqr/dot_general | solution.py:44
  151.3 1.4 fusion
  152.6 1.8 %fusion.17 = f32[4,64,512]{2,1,0:T(8,128)S(1)} fusion(f32[4,64,512]{2,1,0:T(8,128)S(1)} %fusion.28, bf16[768,4,64]{0,2,1:T(8,128)(2,1)S(1)} %bitcast.97, f32[4,768,512]{2,1,0:T(8,128)S(1)} %bitcast.92, f32[4,512]{1,0:T(4,128)S(1)} %max.9, pred[512,768]{0,1:T(8,128)(4,1)S(1)} %fusion.13), kind=kOutput, calls=%fused_computation.28 | convolution fusion | flops 207749120 | bytes 8134656 | tf_op jit(solution)/shard_map/hqk,khe->qhe/dot_general | solution.py:63
  154.9 0.8 copy.35
  (56 shorter events, 6.2 us)
Async XLA Ops:
  6.5 22.0 %copy-start = (bf16[1024,1024]{1,0:T(8,128)(2,1)S(1)}, bf16[1024,1024]{1,0:T(8,128)(2,1)}, u32[]{:S(2)}) copy-start(bf16[1024,1024]{1,0:T(8,128)(2,1)} %param.10) | copy-start | bytes 6291460
  6.5 22.0 %all-gather.2.cloned.1.call-start = ((), (), s32[]{:S(2)}) async-start(), calls=%async_computation | async-start | bytes 1310720 | tf_op jit(solution)/shard_map/all_gather | solution.py:90
  7.3 129.0 %all-reduce.2.cloned.1.call-start = ((), (), s32[]{:S(2)}) async-start(), calls=%async_computation.1 | async-start | bytes 2097152 | tf_op jit(solution)/shard_map/psum | solution.py:119
  9.0 56.1 %collective-permute-start.1 = (bf16[2,128,256]{2,1,0:T(8,128)(2,1)}, bf16[2,128,256]{2,1,0:T(8,128)(2,1)}, u32[]{:S(2)}, u32[]{:S(2)}) collective-permute-start(bf16[2,128,256]{2,1,0:T(8,128)(2,1)} %get-tuple-element.13), channel_id=1, source_target_pairs={{4,0},{8,4},{12,8},{16,12},{20,16},{24,20},{28,24},{5,1},{9,5},{13... | collective-permute-start | bytes 393224 | tf_op jit(solution)/shard_map/ppermute | solution.py:23
  10.3 53.8 %collective-permute-start = (bf16[2,128,256]{2,1,0:T(8,128)(2,1)}, bf16[2,128,256]{2,1,0:T(8,128)(2,1)}, u32[]{:S(2)}, u32[]{:S(2)}) collective-permute-start(bf16[2,128,256]{2,1,0:T(8,128)(2,1)} %get-tuple-element.14), channel_id=1, source_target_pairs={{0,4},{4,8},{8,12},{12,16},{16,20},{20,24},{24,28},{1,5},{5,9},{9,... | collective-permute-start | bytes 393224 | tf_op jit(solution)/shard_map/ppermute | solution.py:22
  19.3 38.3 %copy-start.9 = (pred[512]{0:T(512)(128)(4,1)}, pred[512]{0:T(512)(128)(4,1)S(1)}, u32[]{:S(2)}) copy-start(pred[512]{0:T(512)(128)(4,1)S(1)} %broadcast_compare_fusion) | copy-start | bytes 1540
  57.6 1.5 copy-start.4
  60.3 2.3 %copy-start.11 = (f32[2,256]{1,0:T(2,128)S(1)}, f32[2,256]{1,0:T(2,128)}, u32[]{:S(2)}) copy-start(f32[2,256]{1,0:T(2,128)} %param.11) | copy-start | bytes 6148
  60.3 3.0 %copy-start.12 = (f32[2,256]{1,0:T(2,128)S(1)}, f32[2,256]{1,0:T(2,128)}, u32[]{:S(2)}) copy-start(f32[2,256]{1,0:T(2,128)} %param.12) | copy-start | bytes 6148
  60.3 3.6 %copy-start.6 = (bf16[512,256]{1,0:T(8,128)(2,1)S(1)}, bf16[512,256]{1,0:T(8,128)(2,1)}, u32[]{:S(2)}) copy-start(bf16[512,256]{1,0:T(8,128)(2,1)} %param.8) | copy-start | bytes 786436
  61.8 3.3 %copy-start.2 = (bf16[2,512,256]{2,1,0:T(8,128)(2,1)S(1)}, bf16[2,512,256]{2,1,0:T(8,128)(2,1)}, u32[]{:S(2)}) copy-start(bf16[2,512,256]{2,1,0:T(8,128)(2,1)} %param.9) | copy-start | bytes 1572868
  64.1 5.0 %copy-start.3 = (bf16[512,256]{0,1:T(8,128)(2,1)}, bf16[512,256]{0,1:T(8,128)(2,1)S(1)}, u32[]{:S(2)}) copy-start(bf16[512,256]{0,1:T(8,128)(2,1)S(1)} %copy.22) | copy-start | bytes 786436
  136.3 8.0 %copy-start.1 = (f32[2048,128]{0,1:T(8,128)S(1)}, f32[2048,128]{0,1:T(8,128)}, u32[]{:S(2)}) copy-start(f32[2048,128]{0,1:T(8,128)} %all-reduce.2.cloned.1.call-done) | copy-start | bytes 3145732
  141.0 5.0 %copy-start.7 = (f32[2,4,256,2]{2,0,1,3:T(2,128)S(1)}, f32[2,4,256,2]{2,0,1,3:T(2,128)}, u32[]{:S(2)}) copy-start(f32[2,4,256,2]{2,0,1,3:T(2,128)} %copy.28) | copy-start | bytes 49156
  147.7 1.9 %copy-start.10 = (pred[512]{0:T(512)(128)(4,1)S(1)}, pred[512]{0:T(512)(128)(4,1)}, u32[]{:S(2)}) copy-start(pred[512]{0:T(512)(128)(4,1)} %copy-done.9) | copy-start | bytes 1540
  147.7 3.4 %slice-start = ((s8[6291456]{0:T(1024)(128)(4,1)}), s8[4194304]{0:T(1024)(128)(4,1)S(1)}, s32[]{:S(2)}) async-start(s8[6291456]{0:T(1024)(128)(4,1)} %bitcast.91), calls=%async_computation.2 | async-start | bytes 8388608
  149.6 0.7 copy-start.8
  149.6 1.7 %slice-start.1 = ((s8[6291456]{0:T(1024)(128)(4,1)}), s8[2097152]{0:T(1024)(128)(4,1)S(1)}, s32[]{:S(2)}) async-start(s8[6291456]{0:T(1024)(128)(4,1)} %bitcast.91), calls=%async_computation.3 | async-start | bytes 4194304
  151.3 1.4 copy-start.5
Sparse Core Ops, SparseCore 0:
  8.9 19.5 all-gather.1
  62.0 74.2 all-reduce.1
where the time goes:
time: 163 us
  waiting for transfers between devices  72.7 us (45%)
  local copies, waits for them, and re-layouts  22.3 us (14%)
  blocking collectives  21.6 us (13%)
  between operations  13.7 us (8%)
  matrix products  13.4 us (8%)
  other arithmetic  11.4 us (7%)
  starting transfers between devices  7.45 us (5%)
    psum x1, waiting for transfers between devices, on_device(): summed = lax.psum(numerator, 'seq')  62.8 us
    pmax x1, blocking collectives, on_device(): slot_top = lax.pmax(jnp.stack([first_top, other_top]), 'seq')  21.6 us
    all_gather x1, waiting for transfers between devices, on_device(): lax.all_gather(inputs, 'doc', axis=1, tiled=True)  9.19 us
    ppermute x1, starting transfers between devices, extended(): before = lax.ppermute(last, axis, up)  6.13 us
    dot_general x1, matrix products, attend(): jnp.einsum('qhe,khe->hqk', query_block, window[0], preferred_element_type...  4.49 us
    dot_general x1, matrix products, on_device(): jnp.dot(lax.all_gather(inputs, 'doc', axis=1, tiled=True), slot_weight, p...  3.89 us
    unnamed x34, local copies, waits for them, and re-layouts  3.69 us
  transfers between devices with their start and end apart: 4, of which 2 were waited for; matrix products, arithmetic and copies ran while one was open for 17% of the time, Pallas kernels for 0%

commit v1 on v0

v1 whole, which is shorter than its diff:
```python
import functools

import jax
import jax.numpy as jnp
from jax import lax
from jax.experimental import pallas as pl
from jax.experimental.pallas import tpu as pltpu
from jax.sharding import PartitionSpec as P

DH = 64
R = 256
W = 128
DOCS = 2
CHUNKS = 2
EPSILON = 1e-05
LOW = -1e30
MESH = pl.DeviceIdType.MESH
F32 = jnp.float32
BF16 = jnp.bfloat16

NT = (((1,), (1,)), ((), ()))


def kernel(
    n, nd,
    x_ref, q_ref, kv_ref, w_ref, gain_ref, bias_ref, bounds_ref,
    out_ref,
    xg, wv, qv, kvx, kvm, acc, part, tops, rbuf, rtop, tab,
    gcol, bcol, nbias, nacc, nmax, nsum,
    loc_sem, far_send, far_recv, pair_send, pair_recv, fwd_send, fwd_recv,
    halo_send, halo_recv, part_send, part_recv, top_send, top_recv,
    tab_send, tab_recv,
):
    T, F = x_ref.shape
    heads = q_ref.shape[1] // DH
    blocks = DOCS * heads
    stride = n // blocks
    me = lax.axis_index("seq")
    c = lax.axis_index("doc")
    pc = c + 1 - 2 * lax.rem(c, 2)
    rows = T // CHUNKS

    barrier = pltpu.get_barrier_semaphore()

    def greet(d, carry):
        pl.semaphore_signal(
            barrier, inc=1, device_id={"seq": lax.rem(me + d, n), "doc": c}, device_id_type=MESH
        )
        return carry

    lax.fori_loop(1, n, greet, 0)
    for d in range(1, nd):
        pl.semaphore_signal(
            barrier, inc=1, device_id={"seq": me, "doc": lax.rem(c + d, nd)}, device_id_type=MESH
        )

    cp_x = pltpu.make_async_copy(x_ref, xg.at[c], loc_sem.at[0])
    cp_w = pltpu.make_async_copy(w_ref, wv, loc_sem.at[1])
    cp_q = pltpu.make_async_copy(q_ref, qv, loc_sem.at[2])
    cp_kv = pltpu.make_async_copy(kv_ref, kvx.at[:, pl.ds(W, T), :], loc_sem.at[3])
    for cp in (cp_x, cp_w, cp_kv, cp_q):
        cp.start()

    pl.semaphore_wait(barrier, n - 1 + nd - 1)

    def remote(src, dst, send, recv, seq, doc):
        return pltpu.make_async_remote_copy(
            src_ref=src, dst_ref=dst, send_sem=send, recv_sem=recv,
            device_id={"seq": seq, "doc": doc}, device_id_type=MESH,
        )

    far = []
    for k in range(1, nd // 2):
        for j in range(CHUNKS):
            part_rows = pl.ds(j * rows, rows)
            cp = remote(
                x_ref.at[part_rows], xg.at[c, part_rows],
                far_send.at[k, j], far_recv.at[k, j], me, lax.rem(c + 2 * k, nd),
            )
            cp.start()
            far.append((k, j, cp))
    cp_pair = remote(x_ref, xg.at[c], pair_send, pair_recv, me, pc)
    cp_pair.start()

    up = remote(
        kv_ref.at[:, pl.ds(T - W, W), :], kvx.at[:, pl.ds(0, W), :],
        halo_send.at[0], halo_recv.at[0], lax.rem(me + 1, n), c,
    )
    down = remote(
        kv_ref.at[:, pl.ds(0, W), :], kvx.at[:, pl.ds(T + W, W), :],
        halo_send.at[1], halo_recv.at[1], lax.rem(me + n - 1, n), c,
    )

    @pl.when(me < n - 1)
    def _():
        up.start()

    @pl.when(me > 0)
    def _():
        down.start()

    @pl.when(me == 0)
    def _():
        kvx[:, 0:W, :] = jnp.zeros((2, W, F), BF16)

    @pl.when(me == n - 1)
    def _():
        kvx[:, T + W : T + 2 * W, :] = jnp.zeros((2, W, F), BF16)

    lower = bounds_ref[0, 0]
    split = jnp.where(lower > 0, lower, bounds_ref[1, 0])
    root = me * T
    row_pos = root + lax.broadcasted_iota(jnp.int32, (T, 1), 0)
    second = row_pos >= split

    def w_rows(i):
        return wv[pl.ds(pl.multiple_of(i * F, F), F), :]

    cp_x.wait()
    cp_w.wait()
    acc[...] = jnp.dot(xg[c], w_rows(c), preferred_element_type=F32)
    cp_pair.wait_recv()
    acc[...] += jnp.dot(xg[pc], w_rows(pc), preferred_element_type=F32)

    cp_kv.wait()
    lane_pos = root + lax.broadcasted_iota(jnp.int32, (1, T), 1)
    lane_second = lane_pos >= split
    for s in range(2):
        turned = jnp.transpose(kvx[s, W : W + T, :].astype(F32))
        first_doc = jnp.where(lane_second, 0.0, turned).astype(BF16)
        other_doc = jnp.where(lane_second, turned, 0.0).astype(BF16)
        for h in range(heads):
            kvm[h, 0, s] = first_doc[h * DH : (h + 1) * DH]
            kvm[h, 1, s] = other_doc[h * DH : (h + 1) * DH]

    fwd = []
    for k, j, cp in far:
        cp.wait_recv()
        src = lax.rem(c - 2 * k + nd, nd)
        part_rows = pl.ds(j * rows, rows)
        cp2 = remote(
            xg.at[src, part_rows], xg.at[src, part_rows],
            fwd_send.at[k, j], fwd_recv.at[k, j], me, pc,
        )
        cp2.start()
        fwd.append(cp2)
    for k in range(1, nd // 2):
        src = lax.rem(c - 2 * k + nd, nd)
        acc[...] += jnp.dot(xg[src], w_rows(src), preferred_element_type=F32)
    for cp2 in fwd:
        cp2.wait_recv()
    for k in range(1, nd // 2):
        src = lax.rem(pc - 2 * k + nd, nd)
        acc[...] += jnp.dot(xg[src], w_rows(src), preferred_element_type=F32)

    sends = []
    for h in range(heads):
        logits = acc[:, h * R : (h + 1) * R]
        top0 = jnp.max(jnp.where(second, LOW, logits), axis=0, keepdims=True)
        top1 = jnp.max(jnp.where(second, logits, LOW), axis=0, keepdims=True)
        proj = jnp.exp(logits - jnp.where(second, top1, top0)).astype(BF16)
        sums = jnp.dot(
            kvm[h].reshape(DOCS * 2 * DH, T), proj, preferred_element_type=F32
        ).reshape(DOCS, 2, DH, R)
        sums = sums - jnp.mean(sums, axis=2, keepdims=True)
        for g, top in ((0, top0), (1, top1)):
            b = g * heads + h
            owner = b * stride
            slot = lax.rem(me - owner + n, n)
            tops[b] = jnp.broadcast_to(top, (8, R))
            part[b] = sums[g].astype(BF16)
            send_top = remote(
                tops.at[b], rtop.at[slot], top_send.at[b], top_recv.at[slot], owner, c
            )
            send_part = remote(
                part.at[b], rbuf.at[slot], part_send.at[b], part_recv.at[slot], owner, c
            )
            sends.append((owner, send_top, send_part))

            @pl.when(me != owner)
            def _():
                send_top.start()
                send_part.start()

    diagonal = lax.broadcasted_iota(jnp.int32, (F, F), 0) == lax.broadcasted_iota(
        jnp.int32, (F, F), 1
    )
    for s in range(2):
        for ref, col in ((gain_ref, gcol), (bias_ref, bcol)):
            value = jnp.sum(jnp.where(diagonal, ref[s : s + 1, :], 0.0), axis=1, keepdims=True)
            col[s] = jnp.broadcast_to(value, (F, 128))

    total = n * T
    for b in range(T // W):
        q_pos = root + b * W + lax.broadcasted_iota(jnp.int32, (W, 3 * W), 0)
        k_pos = root + (b - 1) * W + lax.broadcasted_iota(jnp.int32, (W, 3 * W), 1)
        low = jnp.maximum(q_pos - W, jnp.where(q_pos >= split, split, 0))
        high = jnp.minimum(q_pos + W + 1, jnp.where(q_pos >= split, total, split))
        nbias[b] = jnp.where((k_pos >= low) & (k_pos < high), 0.0, LOW)

    cp_q.wait()

    @pl.when(me > 0)
    def _():
        up.wait_recv()

    @pl.when(me < n - 1)
    def _():
        down.wait_recv()

    half = lax.broadcasted_iota(jnp.int32, (1, 2 * DH), 1) // DH

    def query(h, start, size):
        p = h // 2
        q = qv[start : start + size, p * 2 * DH : (p + 1) * 2 * DH] * jnp.asarray(0.125, BF16)
        return jnp.where(half == h % 2, q, jnp.zeros((), BF16))

    def near(h):
        p = h // 2
        lanes = slice(p * 2 * DH, (p + 1) * 2 * DH)
        for b in range(T // W):
            keys = kvx[0, b * W : (b + 3) * W, lanes]
            values = kvx[1, b * W : (b + 3) * W, lanes]
            scores = lax.dot_general(query(h, b * W, W), keys, NT, preferred_element_type=F32)
            scores = scores + nbias[b]
            top = jnp.max(scores, axis=1, keepdims=True)
            weight = jnp.exp(scores - top)
            at = slice(b * W, (b + 1) * W)
            nmax[h, at] = top
            nsum[h, at] = jnp.sum(weight, axis=1, keepdims=True)
            nacc[h, at] = jnp.dot(weight.astype(BF16), values, preferred_element_type=F32)

    for h in range(heads // 2):
        near(h)

    mine = me // stride

    def reduce_block():
        rbuf[0] = part[mine]
        rtop[0] = tops[mine]

        def wait_in(d, top):
            remote(
                tops.at[0], rtop.at[d], top_send.at[0], top_recv.at[d], me, pc
            ).wait_recv()
            remote(
                part.at[0], rbuf.at[d], part_send.at[0], part_recv.at[d], me, pc
            ).wait_recv()
            return jnp.maximum(top, rtop[d])

        top = lax.fori_loop(1, n, wait_in, rtop[0], unroll=n <= 8)[0:1]

        def add(d, running):
            scale = jnp.exp(rtop[d][0:1] - top)
            return running + rbuf[d].astype(F32) * scale[None]

        summed = lax.fori_loop(0, n, add, jnp.zeros((2, DH, R), F32), unroll=n <= 8)
        centred = summed - jnp.mean(summed, axis=1, keepdims=True)
        variance = jnp.mean(centred * centred, axis=1, keepdims=True)
        scaled = centred * lax.rsqrt(variance + EPSILON)
        at = pl.ds(pl.multiple_of(lax.rem(mine, heads) * DH, DH), DH)
        for s in range(2):
            gain = gcol[s, at, :][:, 0:1]
            bias = bcol[s, at, :][:, 0:1]
            tab[mine, s] = (scaled[s] * gain + bias).astype(BF16)

        def spread(d, carry):
            remote(
                tab.at[mine], tab.at[mine], tab_send.at[d], tab_recv.at[mine],
                lax.rem(me + d, n), c,
            ).start()
            return carry

        lax.fori_loop(1, n, spread, 0)

    def finish_spread():
        def done(d, carry):
            remote(
                tab.at[mine], tab.at[mine], tab_send.at[d], tab_recv.at[mine],
                lax.rem(me + d, n), c,
            ).wait_send()
            return carry

        lax.fori_loop(1, n, done, 0)

    if stride == 1 and n == blocks:
        reduce_block()
    else:
        pl.when((lax.rem(me, stride) == 0) & (mine < blocks))(reduce_block)

    for h in range(heads // 2, heads):
        near(h)

    for b in range(blocks):
        @pl.when(me != b * stride)
        def _():
            remote(
                tab.at[b], tab.at[b], tab_send.at[0], tab_recv.at[b], me, pc
            ).wait_recv()

    for p in range(heads // 2):
        keys = [
            tab[g * heads + 2 * p : g * heads + 2 * p + 2, 0].reshape(2 * DH, R)
            for g in range(DOCS)
        ]
        values = [
            tab[g * heads + 2 * p : g * heads + 2 * p + 2, 1].reshape(2 * DH, R)
            for g in range(DOCS)
        ]
        halves = []
        for h in (2 * p, 2 * p + 1):
            q = query(h, 0, T)
            scores = jnp.where(
                second,
                jnp.dot(q, keys[1], preferred_element_type=F32),
                jnp.dot(q, keys[0], preferred_element_type=F32),
            )
            near_top = nmax[h]
            top = jnp.maximum(near_top, jnp.max(scores, axis=1, keepdims=True))
            weight = jnp.exp(scores - top)
            shrink = jnp.exp(near_top - top)
            denominator = nsum[h] * shrink + jnp.sum(weight, axis=1, keepdims=True)
            weight = weight.astype(BF16)
            zero = jnp.zeros((), BF16)
            result = nacc[h] * shrink
            result += lax.dot_general(
                jnp.where(second, zero, weight), values[0], NT, preferred_element_type=F32
            )
            result += lax.dot_general(
                jnp.where(second, weight, zero), values[1], NT, preferred_element_type=F32
            )
            halves.append(result / denominator)
        out_ref[:, p * 2 * DH : (p + 1) * 2 * DH] = jnp.where(
            half == 0, halves[0], halves[1]
        ).astype(out_ref.dtype)

    for _, _, cp in far:
        cp.wait_send()
    cp_pair.wait_send()
    for cp2 in fwd:
        cp2.wait_send()

    @pl.when(me < n - 1)
    def _():
        up.wait_send()

    @pl.when(me > 0)
    def _():
        down.wait_send()

    for owner, send_top, send_part in sends:
        @pl.when(me != owner)
        def _():
            send_top.wait_send()
            send_part.wait_send()

    if stride == 1 and n == blocks:
        finish_spread()
    else:
        pl.when((lax.rem(me, stride) == 0) & (mine < blocks))(finish_spread)


def on_device(n, nd, inputs, queries, keys_values, slot_weight, slot_gain, slot_bias, bounds):
    T, F = inputs.shape
    heads = queries.shape[1] // DH
    blocks = DOCS * heads
    DMA = pltpu.SemaphoreType.DMA
    anywhere = pl.BlockSpec(memory_space=pl.ANY)
    vmem = pl.BlockSpec(memory_space=pltpu.VMEM)
    return pl.pallas_call(
        functools.partial(kernel, n, nd),
        out_shape=jax.ShapeDtypeStruct(queries.shape, BF16),
        in_specs=[anywhere] * 4 + [vmem] * 2 + [pl.BlockSpec(memory_space=pltpu.SMEM)],
        out_specs=vmem,
        scratch_shapes=[
            pltpu.VMEM((nd, T, F), BF16),
            pltpu.VMEM(slot_weight.shape, BF16),
            pltpu.VMEM(queries.shape, BF16),
            pltpu.VMEM((2, T + 2 * W, F), BF16),
            pltpu.VMEM((heads, DOCS, 2, DH, T), BF16),
            pltpu.VMEM((T, heads * R), F32),
            pltpu.VMEM((blocks, 2, DH, R), BF16),
            pltpu.VMEM((blocks, 8, R), F32),
            pltpu.VMEM((n, 2, DH, R), BF16),
            pltpu.VMEM((n, 8, R), F32),
            pltpu.VMEM((blocks, 2, DH, R), BF16),
            pltpu.VMEM((2, F, 128), F32),
            pltpu.VMEM((2, F, 128), F32),
            pltpu.VMEM((T // W, W, 3 * W), F32),
            pltpu.VMEM((heads, T, 2 * DH), F32),
            pltpu.VMEM((heads, T, 1), F32),
            pltpu.VMEM((heads, T, 1), F32),
            DMA((4,)),
            DMA((nd, CHUNKS)), DMA((nd, CHUNKS)),
            DMA, DMA,
            DMA((nd, CHUNKS)), DMA((nd, CHUNKS)),
            DMA((2,)), DMA((2,)),
            DMA((blocks,)), DMA((n,)),
            DMA((blocks,)), DMA((n,)),
            DMA((n,)), DMA((blocks,)),
        ],
        compiler_params=pltpu.CompilerParams(
            collective_id=0, has_side_effects=True, vmem_limit_bytes=48 * 1024 * 1024
        ),
        cost_estimate=pl.CostEstimate(
            flops=4 * 10**9, bytes_accessed=4 * 10**6, transcendentals=2 * 10**6
        ),
    )(inputs, queries, keys_values, slot_weight, slot_gain, slot_bias, bounds)


def solution(mesh):
    return jax.shard_map(
        functools.partial(on_device, mesh.shape["seq"], mesh.shape["doc"]),
        mesh=mesh,
        in_specs=(
            P("seq", "doc"),
            P("seq", "doc"),
            P(None, "seq", "doc"),
            P(None, "doc"),
            P(None, "doc"),
            P(None, "doc"),
            P(None, "seq"),
        ),
        out_specs=P("seq", "doc"),
        check_vma=False,
    )
```

time: 163 us -> 53.4 us (0.33)
  the two profiles are of different devices: /device:TPU:0 before, /device:TPU:27 now
where the time goes in v1:
time: 53.4 us; the launch traced here: 53.1 us
  Pallas kernels  45.8 us (86%)
  local copies, waits for them, and re-layouts  7.28 us (14%)
    pallas_call x1, Pallas kernels, on_device(): pl.pallas_call(functools.partial(kernel, n, nd), out_shape=jax.ShapeDtype...  45.8 us
    unnamed x15, local copies, waits for them, and re-layouts  7.28 us

profile of v1, /device:TPU:27, one launch (start us, length us, event | category | flops | bytes accessed | tf_op | source)
XLA Modules:
  0.0 53.1 jit_solution(12740271166599730203)
XLA Ops:
  0.0 0.0 copy-start
  0.0 1.6 %copy-done = bf16[1024,1024]{1,0:T(8,128)(2,1)S(1)} copy-done((bf16[1024,1024]{1,0:T(8,128)(2,1)S(1)}, bf16[1024,1024]{1,0:T(8,128)(2,1)}, u32[]{:S(2)}) %copy-start) | copy-done | bytes 2097176
  1.6 0.0 copy-start.1
  1.6 1.0 %copy-done.1 = bf16[2,512,256]{2,1,0:T(8,128)(2,1)S(1)} copy-done((bf16[2,512,256]{2,1,0:T(8,128)(2,1)S(1)}, bf16[2,512,256]{2,1,0:T(8,128)(2,1)}, u32[]{:S(2)}) %copy-start.1) | copy-done | bytes 524312
  2.6 0.0 copy-start.2
  2.6 0.9 %copy-done.2 = bf16[512,256]{1,0:T(8,128)(2,1)S(1)} copy-done((bf16[512,256]{1,0:T(8,128)(2,1)S(1)}, bf16[512,256]{1,0:T(8,128)(2,1)}, u32[]{:S(2)}) %copy-start.2) | copy-done | bytes 262168
  3.6 0.0 copy-start.3
  3.6 0.9 %copy-done.3 = bf16[512,256]{1,0:T(8,128)(2,1)S(1)} copy-done((bf16[512,256]{1,0:T(8,128)(2,1)S(1)}, bf16[512,256]{1,0:T(8,128)(2,1)}, u32[]{:S(2)}) %copy-start.3) | copy-done | bytes 262168
  4.5 0.0 copy-start.4
  4.5 0.7 %copy-done.4 = s32[2,512]{1,0:T(2,128)S(1)} copy-done((s32[2,512]{1,0:T(2,128)S(1)}, s32[2,512]{1,0:T(2,128)}, u32[]{:S(2)}) %copy-start.4) | copy-done | bytes 4120
  5.2 0.0 copy-start.5
  5.2 0.7 %copy-done.5 = f32[2,256]{1,0:T(2,128)S(1)} copy-done((f32[2,256]{1,0:T(2,128)S(1)}, f32[2,256]{1,0:T(2,128)}, u32[]{:S(2)}) %copy-start.5) | copy-done | bytes 2072
  5.9 0.0 copy-start.6
  5.9 0.7 %copy-done.6 = f32[2,256]{1,0:T(2,128)S(1)} copy-done((f32[2,256]{1,0:T(2,128)S(1)}, f32[2,256]{1,0:T(2,128)}, u32[]{:S(2)}) %copy-start.6) | copy-done | bytes 2072
  6.6 45.8 %shard_map.73 = bf16[512,256]{1,0:T(8,128)(2,1)S(1)} custom-call(bf16[512,256]{1,0:T(8,128)(2,1)S(1)} %copy-done.2, bf16[512,256]{1,0:T(8,128)(2,1)S(1)} %copy-done.3, bf16[2,512,256]{2,1,0:T(8,128)(2,1)S(1)} %copy-done.1, bf16[1024,1024]{1,0:T(8,128)(2,1)S(1)} %copy-done, f32[2,256]{1,0:T(2,128)S(1)} %copy-done.5, f32[2,256]{1,0:T(2,128)S(1)} %copy-done.6, ...), custom_call_target="tpu_custom_call" | custom-call | flops 4000000000 | bytes 4000000 | tf_op jit(solution)/shard_map/pallas_call | solution.py:370
  52.4 0.7 %copy.9 = bf16[512,256]{1,0:T(8,128)(2,1)} copy(bf16[512,256]{1,0:T(8,128)(2,1)S(1)} %shard_map.73) | data formatting | bytes 524288
Async XLA Ops:
  0.0 1.6 %copy-start = (bf16[1024,1024]{1,0:T(8,128)(2,1)S(1)}, bf16[1024,1024]{1,0:T(8,128)(2,1)}, u32[]{:S(2)}) copy-start(bf16[1024,1024]{1,0:T(8,128)(2,1)} %w_ref.1) | copy-start | bytes 6291460
  1.6 1.0 %copy-start.1 = (bf16[2,512,256]{2,1,0:T(8,128)(2,1)S(1)}, bf16[2,512,256]{2,1,0:T(8,128)(2,1)}, u32[]{:S(2)}) copy-start(bf16[2,512,256]{2,1,0:T(8,128)(2,1)} %kv_ref.1) | copy-start | bytes 1572868
  2.6 0.9 %copy-start.2 = (bf16[512,256]{1,0:T(8,128)(2,1)S(1)}, bf16[512,256]{1,0:T(8,128)(2,1)}, u32[]{:S(2)}) copy-start(bf16[512,256]{1,0:T(8,128)(2,1)} %x_ref.1) | copy-start | bytes 786436
  3.6 0.9 %copy-start.3 = (bf16[512,256]{1,0:T(8,128)(2,1)S(1)}, bf16[512,256]{1,0:T(8,128)(2,1)}, u32[]{:S(2)}) copy-start(bf16[512,256]{1,0:T(8,128)(2,1)} %q_ref.1) | copy-start | bytes 786436
  4.5 0.7 %copy-start.4 = (s32[2,512]{1,0:T(2,128)S(1)}, s32[2,512]{1,0:T(2,128)}, u32[]{:S(2)}) copy-start(s32[2,512]{1,0:T(2,128)} %bounds_ref.1) | copy-start | bytes 12292
  5.2 0.7 %copy-start.5 = (f32[2,256]{1,0:T(2,128)S(1)}, f32[2,256]{1,0:T(2,128)}, u32[]{:S(2)}) copy-start(f32[2,256]{1,0:T(2,128)} %gain_ref.1) | copy-start | bytes 6148
  5.9 0.7 %copy-start.6 = (f32[2,256]{1,0:T(2,128)S(1)}, f32[2,256]{1,0:T(2,128)}, u32[]{:S(2)}) copy-start(f32[2,256]{1,0:T(2,128)} %bias_ref.1) | copy-start | bytes 6148

commit v2 on v1

--- a/solution.py
+++ b/solution.py
@@ -23,13 +23,14 @@
 
 def kernel(
     n, nd,
-    x_ref, q_ref, kv_ref, w_ref, gain_ref, bias_ref, bounds_ref,
+    x_ref, q_ref, kv_ref, w_ref, gain_hbm, bias_hbm, bounds_hbm,
     out_ref,
+    gain_ref, bias_ref, bounds_ref,
     xg, wv, qv, kvx, kvm, acc, part, tops, rbuf, rtop, tab,
     gcol, bcol, nbias, nacc, nmax, nsum,
     loc_sem, far_send, far_recv, pair_send, pair_recv, fwd_send, fwd_recv,
     halo_send, halo_recv, part_send, part_recv, top_send, top_recv,
-    tab_send, tab_recv,
+    tab_send, tab_recv, hand_send, qdoc,
 ):
     T, F = x_ref.shape
     heads = q_ref.shape[1] // DH
@@ -58,7 +59,10 @@
     cp_w = pltpu.make_async_copy(w_ref, wv, loc_sem.at[1])
     cp_q = pltpu.make_async_copy(q_ref, qv, loc_sem.at[2])
     cp_kv = pltpu.make_async_copy(kv_ref, kvx.at[:, pl.ds(W, T), :], loc_sem.at[3])
-    for cp in (cp_x, cp_w, cp_kv, cp_q):
+    cp_bounds = pltpu.make_async_copy(bounds_hbm, bounds_ref, loc_sem.at[4])
+    cp_gain = pltpu.make_async_copy(gain_hbm, gain_ref, loc_sem.at[5])
+    cp_bias = pltpu.make_async_copy(bias_hbm, bias_ref, loc_sem.at[6])
+    for cp in (cp_x, cp_w, cp_bounds, cp_kv, cp_q, cp_gain, cp_bias):
         cp.start()
 
     pl.semaphore_wait(barrier, n - 1 + nd - 1)
@@ -107,8 +111,9 @@
     def _():
         kvx[:, T + W : T + 2 * W, :] = jnp.zeros((2, W, F), BF16)
 
-    lower = bounds_ref[0, 0]
-    split = jnp.where(lower > 0, lower, bounds_ref[1, 0])
+    cp_bounds.wait()
+    lower = bounds_ref[0:1, 0:1]
+    split = jnp.where(lower > 0, lower, bounds_ref[1:2, 0:1])
     root = me * T
     row_pos = root + lax.broadcasted_iota(jnp.int32, (T, 1), 0)
     second = row_pos >= split
@@ -182,6 +187,8 @@
                 send_top.start()
                 send_part.start()
 
+    cp_gain.wait()
+    cp_bias.wait()
     diagonal = lax.broadcasted_iota(jnp.int32, (F, F), 0) == lax.broadcasted_iota(
         jnp.int32, (F, F), 1
     )
@@ -230,10 +237,20 @@
             nsum[h, at] = jnp.sum(weight, axis=1, keepdims=True)
             nacc[h, at] = jnp.dot(weight.astype(BF16), values, preferred_element_type=F32)
 
-    for h in range(heads // 2):
+    for h in range(heads):
+        query_all = query(h, 0, T)
+        zero = jnp.zeros((), BF16)
+        qdoc[h, :, 0 : 2 * DH] = jnp.where(second, zero, query_all)
+        qdoc[h, :, 2 * DH : 4 * DH] = jnp.where(second, query_all, zero)
         near(h)
 
     mine = me // stride
+    pair = me + 1 - 2 * lax.rem(me, 2)
+
+    def own_block(d, to):
+        return remote(
+            tab.at[mine], tab.at[mine], tab_send.at[d], tab_recv.at[mine], to, c
+        )
 
     def reduce_block():
         rbuf[0] = part[mine]
@@ -265,69 +282,68 @@
             tab[mine, s] = (scaled[s] * gain + bias).astype(BF16)
 
         def spread(d, carry):
-            remote(
-                tab.at[mine], tab.at[mine], tab_send.at[d], tab_recv.at[mine],
-                lax.rem(me + d, n), c,
-            ).start()
+            own_block(d, lax.rem(me + 2 * d, n)).start()
             return carry
 
-        lax.fori_loop(1, n, spread, 0)
+        lax.fori_loop(1, n // 2, spread, 0)
+        own_block(0, pair).start()
 
     def finish_spread():
         def done(d, carry):
-            remote(
-                tab.at[mine], tab.at[mine], tab_send.at[d], tab_recv.at[mine],
-                lax.rem(me + d, n), c,
-            ).wait_send()
+            own_block(d, lax.rem(me + 2 * d, n)).wait_send()
             return carry
 
-        lax.fori_loop(1, n, done, 0)
+        lax.fori_loop(1, n // 2, done, 0)
+        own_block(0, pair).wait_send()
 
     if stride == 1 and n == blocks:
         reduce_block()
     else:
         pl.when((lax.rem(me, stride) == 0) & (mine < blocks))(reduce_block)
 
-    for h in range(heads // 2, heads):
-        near(h)
-
+    handed = []
     for b in range(blocks):
-        @pl.when(me != b * stride)
+        owner = b * stride
+        hand = remote(tab.at[b], tab.at[b], hand_send.at[b], tab_recv.at[b], pair, c)
+        here = (me != owner) & (lax.rem(me + owner, 2) == 0)
+        handed.append((hand, here))
+
+        @pl.when(here)
         def _():
-            remote(
-                tab.at[b], tab.at[b], tab_send.at[0], tab_recv.at[b], me, pc
-            ).wait_recv()
+            hand.wait_recv()
+            hand.start()
+
+    for b in range(blocks):
+        hand, _ = handed[b]
+
+        @pl.when(lax.rem(me + b * stride, 2) == 1)
+        def _():
+            hand.wait_recv()
 
     for p in range(heads // 2):
-        keys = [
-            tab[g * heads + 2 * p : g * heads + 2 * p + 2, 0].reshape(2 * DH, R)
-            for g in range(DOCS)
-        ]
-        values = [
-            tab[g * heads + 2 * p : g * heads + 2 * p + 2, 1].reshape(2 * DH, R)
-            for g in range(DOCS)
+        keys, values = [
+            jnp.concatenate(
+                [
+                    tab[g * heads + 2 * p : g * heads + 2 * p + 2, s].reshape(2 * DH, R)
+                    for g in range(DOCS)
+                ],
+                axis=0,
+            )
+            for s in range(2)
         ]
         halves = []
         for h in (2 * p, 2 * p + 1):
-            q = query(h, 0, T)
-            scores = jnp.where(
-                second,
-                jnp.dot(q, keys[1], preferred_element_type=F32),
-                jnp.dot(q, keys[0], preferred_element_type=F32),
-            )
+            scores = jnp.dot(qdoc[h], keys, preferred_element_type=F32)
             near_top = nmax[h]
             top = jnp.maximum(near_top, jnp.max(scores, axis=1, keepdims=True))
             weight = jnp.exp(scores - top)
             shrink = jnp.exp(near_top - top)
             denominator = nsum[h] * shrink + jnp.sum(weight, axis=1, keepdims=True)
-            weight = weight.astype(BF16)
-            zero = jnp.zeros((), BF16)
-            result = nacc[h] * shrink
-            result += lax.dot_general(
-                jnp.where(second, zero, weight), values[0], NT, preferred_element_type=F32
-            )
-            result += lax.dot_general(
-                jnp.where(second, weight, zero), values[1], NT, preferred_element_type=F32
+            both = lax.dot_general(
+                weight.astype(BF16), values, NT, preferred_element_type=F32
+            )
+            result = nacc[h] * shrink + jnp.where(
+                second, both[:, 2 * DH : 4 * DH], both[:, 0 : 2 * DH]
             )
             halves.append(result / denominator)
         out_ref[:, p * 2 * DH : (p + 1) * 2 * DH] = jnp.where(
@@ -348,6 +364,9 @@
     def _():
         down.wait_send()
 
+    for hand, here in handed:
+        pl.when(here)(hand.wait_send)
+
     for owner, send_top, send_part in sends:
         @pl.when(me != owner)
         def _():
@@ -365,14 +384,17 @@
     heads = queries.shape[1] // DH
     blocks = DOCS * heads
     DMA = pltpu.SemaphoreType.DMA
-    anywhere = pl.BlockSpec(memory_space=pl.ANY)
+    hbm = pl.BlockSpec(memory_space=pltpu.HBM)
     vmem = pl.BlockSpec(memory_space=pltpu.VMEM)
     return pl.pallas_call(
         functools.partial(kernel, n, nd),
         out_shape=jax.ShapeDtypeStruct(queries.shape, BF16),
-        in_specs=[anywhere] * 4 + [vmem] * 2 + [pl.BlockSpec(memory_space=pltpu.SMEM)],
+        in_specs=[hbm] * 7,
         out_specs=vmem,
         scratch_shapes=[
+            pltpu.VMEM(slot_gain.shape, F32),
+            pltpu.VMEM(slot_bias.shape, F32),
+            pltpu.VMEM(bounds.shape, jnp.int32),
             pltpu.VMEM((nd, T, F), BF16),
             pltpu.VMEM(slot_weight.shape, BF16),
             pltpu.VMEM(queries.shape, BF16),
@@ -390,17 +412,18 @@
             pltpu.VMEM((heads, T, 2 * DH), F32),
             pltpu.VMEM((heads, T, 1), F32),
             pltpu.VMEM((heads, T, 1), F32),
-            DMA((4,)),
+            DMA((7,)),
             DMA((nd, CHUNKS)), DMA((nd, CHUNKS)),
             DMA, DMA,
             DMA((nd, CHUNKS)), DMA((nd, CHUNKS)),
             DMA((2,)), DMA((2,)),
             DMA((blocks,)), DMA((n,)),
             DMA((blocks,)), DMA((n,)),
-            DMA((n,)), DMA((blocks,)),
+            DMA((n,)), DMA((blocks,)), DMA((blocks,)),
+            pltpu.VMEM((heads, T, 4 * DH), BF16),
         ],
         compiler_params=pltpu.CompilerParams(
-            collective_id=0, has_side_effects=True, vmem_limit_bytes=48 * 1024 * 1024
+            collective_id=0, has_side_effects=True, vmem_limit_bytes=60 * 1024 * 1024
         ),
         cost_estimate=pl.CostEstimate(
             flops=4 * 10**9, bytes_accessed=4 * 10**6, transcendentals=2 * 10**6

time: 53.4 us -> 47.7 us (0.89)
  the two profiles are of different devices: /device:TPU:27 before, /device:TPU:0 now
where the time goes in v2:
time: 47.7 us; the launch traced here: 47.5 us
  Pallas kernels  45.8 us (96%)
  local copies, waits for them, and re-layouts  1.67 us (4%)
    pallas_call x1, Pallas kernels, on_device(): pl.pallas_call(functools.partial(kernel, n, nd), out_shape=jax.ShapeDtype...  45.8 us
    unnamed x1, local copies, waits for them, and re-layouts  1.67 us

profile of v2, /device:TPU:0, one launch (start us, length us, event | category | flops | bytes accessed | tf_op | source)
XLA Modules:
  0.0 47.5 jit_solution(13879745375993470283)
XLA Ops:
  0.0 45.8 %shard_map.73 = bf16[512,256]{1,0:T(8,128)(2,1)} custom-call(bf16[512,256]{1,0:T(8,128)(2,1)} %x_ref.1, bf16[512,256]{1,0:T(8,128)(2,1)} %q_ref.1, bf16[2,512,256]{2,1,0:T(8,128)(2,1)} %kv_ref.1, bf16[1024,1024]{1,0:T(8,128)(2,1)} %w_ref.1, f32[2,256]{1,0:T(2,128)} %gain_hbm.1, f32[2,256]{1,0:T(2,128)} %bias_hbm.1, s32[2,512]{1,0:T(2,128)} %bounds_hbm.1), custom_call_target="tpu_custom_call" | custom-call | flops 4000000000 | bytes 4000000 | tf_op jit(solution)/shard_map/pallas_call | solution.py:389
  45.9 1.7 %copy.9 = bf16[512,256]{1,0:T(8,128)(2,1)} copy(bf16[512,256]{1,0:T(8,128)(2,1)} %shard_map.73) | data formatting | bytes 524288

commit v3 on v2

--- a/solution.py
+++ b/solution.py
@@ -14,6 +14,7 @@
 CHUNKS = 2
 EPSILON = 1e-05
 LOW = -1e30
+ZONES = 4
 MESH = pl.DeviceIdType.MESH
 F32 = jnp.float32
 BF16 = jnp.bfloat16
@@ -22,7 +23,7 @@
 
 
 def kernel(
-    n, nd,
+    n, nd, zone,
     x_ref, q_ref, kv_ref, w_ref, gain_hbm, bias_hbm, bounds_hbm,
     out_ref,
     gain_ref, bias_ref, bounds_ref,
@@ -30,7 +31,7 @@
     gcol, bcol, nbias, nacc, nmax, nsum,
     loc_sem, far_send, far_recv, pair_send, pair_recv, fwd_send, fwd_recv,
     halo_send, halo_recv, part_send, part_recv, top_send, top_recv,
-    tab_send, tab_recv, hand_send, qdoc,
+    tab_send, tab_recv, qdoc,
 ):
     T, F = x_ref.shape
     heads = q_ref.shape[1] // DH
@@ -40,6 +41,9 @@
     c = lax.axis_index("doc")
     pc = c + 1 - 2 * lax.rem(c, 2)
     rows = T // CHUNKS
+
+    def holds(g, device):
+        return (device // (n // ZONES) - zone) * (1 - 2 * g) <= 0
 
     barrier = pltpu.get_barrier_semaphore()
 
@@ -180,9 +184,10 @@
             send_part = remote(
                 part.at[b], rbuf.at[slot], part_send.at[b], part_recv.at[slot], owner, c
             )
-            sends.append((owner, send_top, send_part))
-
-            @pl.when(me != owner)
+            out = (me != owner) & holds(g, me)
+            sends.append((out, send_top, send_part))
+
+            @pl.when(out)
             def _():
                 send_top.start()
                 send_part.start()
@@ -245,11 +250,12 @@
         near(h)
 
     mine = me // stride
-    pair = me + 1 - 2 * lax.rem(me, 2)
-
-    def own_block(d, to):
+    doc_mine = mine // heads
+
+    def own_block(d):
         return remote(
-            tab.at[mine], tab.at[mine], tab_send.at[d], tab_recv.at[mine], to, c
+            tab.at[mine], tab.at[mine], tab_send.at[d], tab_recv.at[mine],
+            lax.rem(me + d, n), c,
         )
 
     def reduce_block():
@@ -257,12 +263,22 @@
         rtop[0] = tops[mine]
 
         def wait_in(d, top):
-            remote(
-                tops.at[0], rtop.at[d], top_send.at[0], top_recv.at[d], me, pc
-            ).wait_recv()
-            remote(
-                part.at[0], rbuf.at[d], part_send.at[0], part_recv.at[d], me, pc
-            ).wait_recv()
+            held = holds(doc_mine, lax.rem(me + d, n))
+
+            @pl.when(held)
+            def _():
+                remote(
+                    tops.at[0], rtop.at[d], top_send.at[0], top_recv.at[d], me, pc
+                ).wait_recv()
+                remote(
+                    part.at[0], rbuf.at[d], part_send.at[0], part_recv.at[d], me, pc
+                ).wait_recv()
+
+            @pl.when(jnp.logical_not(held))
+            def _():
+                rtop[d] = jnp.full((8, R), LOW, F32)
+                rbuf[d] = jnp.zeros((2, DH, R), BF16)
+
             return jnp.maximum(top, rtop[d])
 
         top = lax.fori_loop(1, n, wait_in, rtop[0], unroll=n <= 8)[0:1]
@@ -282,43 +298,35 @@
             tab[mine, s] = (scaled[s] * gain + bias).astype(BF16)
 
         def spread(d, carry):
-            own_block(d, lax.rem(me + 2 * d, n)).start()
+            pl.when(holds(doc_mine, lax.rem(me + d, n)))(own_block(d).start)
             return carry
 
-        lax.fori_loop(1, n // 2, spread, 0)
-        own_block(0, pair).start()
+        lax.fori_loop(1, n, spread, 0)
 
     def finish_spread():
         def done(d, carry):
-            own_block(d, lax.rem(me + 2 * d, n)).wait_send()
+            pl.when(holds(doc_mine, lax.rem(me + d, n)))(own_block(d).wait_send)
             return carry
 
-        lax.fori_loop(1, n // 2, done, 0)
-        own_block(0, pair).wait_send()
+        lax.fori_loop(1, n, done, 0)
 
     if stride == 1 and n == blocks:
         reduce_block()
     else:
         pl.when((lax.rem(me, stride) == 0) & (mine < blocks))(reduce_block)
 
-    handed = []
     for b in range(blocks):
-        owner = b * stride
-        hand = remote(tab.at[b], tab.at[b], hand_send.at[b], tab_recv.at[b], pair, c)
-        here = (me != owner) & (lax.rem(me + owner, 2) == 0)
-        handed.append((hand, here))
-
-        @pl.when(here)
+        held = holds(b // heads, me)
+
+        @pl.when((me != b * stride) & held)
         def _():
-            hand.wait_recv()
-            hand.start()
-
-    for b in range(blocks):
-        hand, _ = handed[b]
-
-        @pl.when(lax.rem(me + b * stride, 2) == 1)
+            remote(
+                tab.at[b], tab.at[b], tab_send.at[0], tab_recv.at[b], me, pc
+            ).wait_recv()
+
+        @pl.when((me != b * stride) & jnp.logical_not(held))
         def _():
-            hand.wait_recv()
+            tab[b] = jnp.zeros((2, DH, R), BF16)
 
     for p in range(heads // 2):
         keys, values = [
@@ -364,11 +372,8 @@
     def _():
         down.wait_send()
 
-    for hand, here in handed:
-        pl.when(here)(hand.wait_send)
-
-    for owner, send_top, send_part in sends:
-        @pl.when(me != owner)
+    for out, send_top, send_part in sends:
+        @pl.when(out)
         def _():
             send_top.wait_send()
             send_part.wait_send()
@@ -386,8 +391,8 @@
     DMA = pltpu.SemaphoreType.DMA
     hbm = pl.BlockSpec(memory_space=pltpu.HBM)
     vmem = pl.BlockSpec(memory_space=pltpu.VMEM)
-    return pl.pallas_call(
-        functools.partial(kernel, n, nd),
+    call = lambda zone: pl.pallas_call(
+        functools.partial(kernel, n, nd, zone),
         out_shape=jax.ShapeDtypeStruct(queries.shape, BF16),
         in_specs=[hbm] * 7,
         out_specs=vmem,
@@ -419,16 +424,22 @@
             DMA((2,)), DMA((2,)),
             DMA((blocks,)), DMA((n,)),
             DMA((blocks,)), DMA((n,)),
-            DMA((n,)), DMA((blocks,)), DMA((blocks,)),
+            DMA((n,)), DMA((blocks,)),
             pltpu.VMEM((heads, T, 4 * DH), BF16),
         ],
         compiler_params=pltpu.CompilerParams(
-            collective_id=0, has_side_effects=True, vmem_limit_bytes=60 * 1024 * 1024
+            collective_id=zone, has_side_effects=True, vmem_limit_bytes=60 * 1024 * 1024
         ),
         cost_estimate=pl.CostEstimate(
             flops=4 * 10**9, bytes_accessed=4 * 10**6, transcendentals=2 * 10**6
         ),
-    )(inputs, queries, keys_values, slot_weight, slot_gain, slot_bias, bounds)
+    )
+    lower = bounds[0, 0]
+    split = jnp.where(lower > 0, lower, bounds[1, 0])
+    return lax.cond(
+        split <= n * T // 2, call(1), call(2),
+        inputs, queries, keys_values, slot_weight, slot_gain, slot_bias, bounds,
+    )
 
 
 def solution(mesh):

time: 47.7 us -> 37.3 us (0.78)
  the two profiles are of different devices: /device:TPU:0 before, /device:TPU:18 now
where the time goes in v3:
time: 37.3 us; the launch traced here: 36.9 us
  Pallas kernels  32.7 us (88%)
  local copies, waits for them, and re-layouts  2.03 us (5%)
  between operations  1.93 us (5%)
    pallas_call x1, Pallas kernels, on_device(): lax.cond(split <= n * T // 2, call(1), call(2), inputs, queries, keys_val...  32.7 us
    slice x1, local copies, waits for them, and re-layouts, on_device(): split = jnp.where(lower > 0, lower, bounds[1, 0])  1.33 us

profile of v3, /device:TPU:18, one launch (start us, length us, event | category | flops | bytes accessed | tf_op | source)
XLA Modules:
  0.0 36.9 jit_solution(11380105696359856633)
XLA Ops:
  0.0 1.3 %fusion = (s32[1,1]{1,0:T(1,128)}, s32[1,1]{1,0:T(1,128)}) fusion(s32[2,512]{1,0:T(2,128)} %param.15), kind=kLoop, calls=%fused_computation | loop fusion | bytes 16 | tf_op jit(solution)/shard_map/slice | solution.py:438
  3.2 33.0 %conditional.1 = (bf16[512,256]{1,0:T(8,128)(2,1)S(1)}) conditional(s32[]{:T(128)} %convert_element_type.3, (bf16[512,256]{1,0:T(8,128)(2,1)}, bf16[512,256]{1,0:T(8,128)(2,1)}, bf16[2,512,256]{2,1,0:T(8,128)(2,1)}, bf16[1024,1024]{1,0:T(8,128)(2,1)}, f32[2,256]{1,0:T(2,128)}, /*index=5*/f32[2,256]{1,0:T(2,128)}, s32[2,512]{1,0:T(2,128)}) %tuple.11, ...), branch_computations={%region_0.1_spmd, %region_1.2_spmd} | conditional | flops 4000000000 | bytes 4000008 | solution.py:439
  3.3 32.7 %branch_0_fun.1 = bf16[512,256]{1,0:T(8,128)(2,1)S(1)} custom-call(bf16[512,256]{1,0:T(8,128)(2,1)} %get-tuple-element.36.x_ref, bf16[512,256]{1,0:T(8,128)(2,1)} %get-tuple-element.37.q_ref, bf16[2,512,256]{2,1,0:T(8,128)(2,1)} %get-tuple-element.38.kv_ref, bf16[1024,1024]{1,0:T(8,128)(2,1)} %get-tuple-element.39.w_ref, ...), custom_call_target="tpu_custom_call" | custom-call | flops 4000000000 | bytes 4000000 | tf_op jit(solution)/shard_map/cond/branch_0_fun/pallas_call | solution.py:439
  36.2 0.7 %copy.13 = bf16[512,256]{1,0:T(8,128)(2,1)} copy(bf16[512,256]{1,0:T(8,128)(2,1)S(1)} %get-tuple-element.50) | data formatting | bytes 524288

commit v4 on v3

--- a/solution.py
+++ b/solution.py
@@ -242,11 +242,7 @@
             nsum[h, at] = jnp.sum(weight, axis=1, keepdims=True)
             nacc[h, at] = jnp.dot(weight.astype(BF16), values, preferred_element_type=F32)
 
-    for h in range(heads):
-        query_all = query(h, 0, T)
-        zero = jnp.zeros((), BF16)
-        qdoc[h, :, 0 : 2 * DH] = jnp.where(second, zero, query_all)
-        qdoc[h, :, 2 * DH : 4 * DH] = jnp.where(second, query_all, zero)
+    for h in range(heads // 2):
         near(h)
 
     mine = me // stride
@@ -314,6 +310,14 @@
         reduce_block()
     else:
         pl.when((lax.rem(me, stride) == 0) & (mine < blocks))(reduce_block)
+
+    for h in range(heads):
+        query_all = query(h, 0, T)
+        zero = jnp.zeros((), BF16)
+        qdoc[h, :, 0 : 2 * DH] = jnp.where(second, zero, query_all)
+        qdoc[h, :, 2 * DH : 4 * DH] = jnp.where(second, query_all, zero)
+        if h >= heads // 2:
+            near(h)
 
     for b in range(blocks):
         held = holds(b // heads, me)

time: 37.3 us -> 37.2 us (level)
  the two profiles are of different devices: /device:TPU:18 before, /device:TPU:0 now
where the time goes in v4:
time: 37.2 us; the launch traced here: 36.9 us
  Pallas kernels  32.7 us (88%)
  local copies, waits for them, and re-layouts  2.03 us (5%)
  between operations  1.93 us (5%)
    pallas_call x1, Pallas kernels, on_device(): lax.cond(split <= n * T // 2, call(1), call(2), inputs, queries, keys_val...  32.7 us
    slice x1, local copies, waits for them, and re-layouts, on_device(): split = jnp.where(lower > 0, lower, bounds[1, 0])  1.33 us

profile of v4, /device:TPU:0, one launch (start us, length us, event | category | flops | bytes accessed | tf_op | source)
XLA Modules:
  0.0 36.9 jit_solution(15603476534881857944)
XLA Ops:
  0.0 1.3 %fusion = (s32[1,1]{1,0:T(1,128)}, s32[1,1]{1,0:T(1,128)}) fusion(s32[2,512]{1,0:T(2,128)} %param.15), kind=kLoop, calls=%fused_computation | loop fusion | bytes 16 | tf_op jit(solution)/shard_map/slice | solution.py:442
  3.2 32.9 %conditional.1 = (bf16[512,256]{1,0:T(8,128)(2,1)S(1)}) conditional(s32[]{:T(128)} %convert_element_type.3, (bf16[512,256]{1,0:T(8,128)(2,1)}, bf16[512,256]{1,0:T(8,128)(2,1)}, bf16[2,512,256]{2,1,0:T(8,128)(2,1)}, bf16[1024,1024]{1,0:T(8,128)(2,1)}, f32[2,256]{1,0:T(2,128)}, /*index=5*/f32[2,256]{1,0:T(2,128)}, s32[2,512]{1,0:T(2,128)}) %tuple.11, ...), branch_computations={%region_0.1_spmd, %region_1.2_spmd} | conditional | flops 4000000000 | bytes 4000008 | solution.py:443
  3.3 32.7 %branch_0_fun.1 = bf16[512,256]{1,0:T(8,128)(2,1)S(1)} custom-call(bf16[512,256]{1,0:T(8,128)(2,1)} %get-tuple-element.36.x_ref, bf16[512,256]{1,0:T(8,128)(2,1)} %get-tuple-element.37.q_ref, bf16[2,512,256]{2,1,0:T(8,128)(2,1)} %get-tuple-element.38.kv_ref, bf16[1024,1024]{1,0:T(8,128)(2,1)} %get-tuple-element.39.w_ref, ...), custom_call_target="tpu_custom_call" | custom-call | flops 4000000000 | bytes 4000000 | tf_op jit(solution)/shard_map/cond/branch_0_fun/pallas_call | solution.py:443
  36.2 0.7 %copy.13 = bf16[512,256]{1,0:T(8,128)(2,1)} copy(bf16[512,256]{1,0:T(8,128)(2,1)S(1)} %get-tuple-element.50) | data formatting | bytes 524288
